TPU v7x, 32 devices: a whole 2x2x4 slice. The times are simulated.
32 devices in a mesh: group: 2 (over x), dx: 16 (over z, y, core).
Axes of the slice: x: 2, y: 2, z: 4, core: 2. Of those that a mesh axis runs over, the one named last changes fastest.
Arguments:
- points: bfloat16 [16384, 1024], P(('group', 'dx')), parts along dimension 0, may hold values from -6 to 6
- cotangent: bfloat16 [16384, 1024], P(('group', 'dx')), parts along dimension 0, may hold values from -96 to 96
- counts: int32 [32], P(('group', 'dx')), parts along dimension 0, may hold values from 170 to 512, as said below
- w_query: bfloat16 [1024, 1024], replicated, may hold values from -0.1875 to 0.1875
- w_key: bfloat16 [1024, 1024], replicated, may hold values from -0.1875 to 0.1875
- w_value: bfloat16 [1024, 1024], replicated, may hold values from -0.1875 to 0.1875
- gain_key: float32 [1024], replicated, may hold values from 0.25 to 1.75
- bias_key: float32 [1024], replicated, may hold values from -3 to 3
- gain_value: float32 [1024], replicated, may hold values from 0.25 to 1.75
- bias_value: float32 [1024], replicated, may hold values from -3 to 3
Outputs:
- grad_points: bfloat16 [16384, 1024], P(('group', 'dx')), parts along dimension 0
There are 2 independent parts, one for each index of `group`. A program takes and returns all parts, laid end to end along the dimension named above; an argument that names none is the same for every part. Nothing has to cross between parts.
Inputs may be any that keep to these rules, and one draw needn't show every extreme that they name: `counts`: live points of each tile; some tile of every slab holds 512.
All inputs are finite; a program needn't handle non-finite values.
Results may differ from a plain program's by a relative error of at most 0.006.
Values sent between devices are 32-bit elements; how exact they have to be, the bound alone decides.
A program may use at most 64 MiB of HBM per device.

v0:
```python
import jax
import jax.numpy as jnp
from jax import lax
from jax.sharding import PartitionSpec as P

HEADS = 8


eps = 1e-05


def head_norm(raw, heads):
    grouped = raw.reshape(raw.shape[0], heads, -1)
    center = grouped - jnp.mean(grouped, axis=2, keepdims=True)
    inverse = lax.rsqrt(jnp.mean(center * center, axis=2, keepdims=True) + eps)
    return (center * inverse, inverse)


def norm_back(grad, gain, normed, inverse, heads):
    scaled = grad * gain.reshape(heads, -1)
    inner = scaled - jnp.mean(scaled, axis=2, keepdims=True)
    inner = inner - normed * jnp.mean(scaled * normed, axis=2, keepdims=True)
    return (inverse * inner).reshape(grad.shape[0], -1).astype(jnp.bfloat16)


def body(
    points, cotangent, counts, w_query, w_key, w_value, gain_key, bias_key, gain_value, bias_value
):
    rows = points.shape[0]
    heads = HEADS
    live = (lax.iota(jnp.int32, rows) < counts[0]).astype(jnp.float32)[:, None]
    live_h = live[:, :, None]
    own_count = counts[0].astype(jnp.float32)
    total = lax.psum(own_count, "dx")
    key_hat, key_inv = head_norm(jnp.dot(points, w_key, preferred_element_type=jnp.float32), heads)
    value_hat, value_inv = head_norm(
        jnp.dot(points, w_value, preferred_element_type=jnp.float32), heads
    )
    keys = (live_h * (key_hat * gain_key.reshape(heads, -1) + bias_key.reshape(heads, -1))).astype(
        jnp.bfloat16
    )
    values = (
        live_h * (value_hat * gain_value.reshape(heads, -1) + bias_value.reshape(heads, -1))
    ).astype(jnp.bfloat16)
    kv_local = jnp.einsum("nhi,nhj->hij", keys, values, preferred_element_type=jnp.float32)
    cot = cotangent.reshape(rows, heads, -1)
    kv_sum = lax.psum(kv_local, "dx")
    query = jnp.dot(points, w_query, preferred_element_type=jnp.float32).astype(jnp.bfloat16)
    masked_query = (query * live.astype(jnp.bfloat16)).reshape(rows, heads, -1)
    qdy_local = jnp.einsum("nhi,nhj->hij", masked_query, cot, preferred_element_type=jnp.float32)
    qdy_sum = lax.psum(qdy_local, "dx")
    gram = (kv_sum / total).astype(jnp.bfloat16)
    dgram = (qdy_sum / total).astype(jnp.bfloat16)
    dquery = (
        (live_h * jnp.einsum("nhj,hij->nhi", cot, gram, preferred_element_type=jnp.float32))
        .reshape(rows, -1)
        .astype(jnp.bfloat16)
    )
    dkeys = jnp.einsum("nhj,hij->nhi", values, dgram, preferred_element_type=jnp.float32)
    dvalues = jnp.einsum("nhi,hij->nhj", keys, dgram, preferred_element_type=jnp.float32)
    dkey_raw = norm_back(dkeys, gain_key, key_hat, key_inv, heads)
    dvalue_raw = norm_back(dvalues, gain_value, value_hat, value_inv, heads)
    grad = jnp.dot(dquery, w_query.T, preferred_element_type=jnp.float32)
    grad = grad + jnp.dot(dkey_raw, w_key.T, preferred_element_type=jnp.float32)
    grad = grad + jnp.dot(dvalue_raw, w_value.T, preferred_element_type=jnp.float32)
    return grad.astype(jnp.bfloat16)


def solution(mesh):
    placed = (
        P(("group", "dx"), None),
        P(("group", "dx"), None),
        P(("group", "dx")),
        P(),
        P(),
        P(),
        P(),
        P(),
        P(),
        P(),
    )
    return jax.shard_map(
        body, mesh=mesh, in_specs=placed, out_specs=P(("group", "dx"), None), check_vma=False
    )
```

profile of v0, /device:TPU:0, one launch (start us, length us, event | category | flops | bytes accessed | tf_op | source)
XLA Modules:
  0.0 156.2 jit_solution(9435731812244880489)
XLA Ops:
  6.5 3.3 %convolution_bitcast_fusion = f32[64,8,8,128]{3,1,2,0:T(8,128)S(1)} fusion(bf16[512,1024]{1,0:T(8,128)(2,1)} %param.10, bf16[1024,1024]{1,0:T(8,128)(2,1)} %param.15), kind=kOutput, calls=%fused_computation.22 | convolution fusion | flops 1073741824 | bytes 5242880 | tf_op jit(solution)/shard_map/dot_general | solution.py:37
  9.8 1.8 %copy.72 = f32[64,8,8,128]{3,2,1,0:T(8,128)} copy(f32[64,8,8,128]{3,1,2,0:T(8,128)S(1)} %convolution_bitcast_fusion) | data formatting | bytes 4194304
  11.6 3.0 %copy.57 = f32[512,8,128]{0,2,1:T(8,128)} copy(f32[512,8,128]{2,1,0:T(8,128)} %bitcast.70) | data formatting | bytes 4194304 | tf_op jit(solution)/shard_map/reshape | solution.py:13
  14.6 2.3 %reduce_sum.74 = f32[512,8]{1,0:T(8,128)S(1)} reduce(f32[512,8,128]{2,1,0:T(8,128)} %bitcast.71, f32[]{:T(128)} %constant.11.clone.1), dimensions={2}, to_apply=%region_2.0 | reduce | flops 520192 | bytes 2113540 | tf_op jit(solution)/shard_map/reduce_sum | solution.py:14
  16.9 1.3 convolution_bitcast_fusion.1
  18.2 1.8 %copy.71 = f32[64,8,8,128]{3,2,1,0:T(8,128)} copy(f32[64,8,8,128]{3,1,2,0:T(8,128)S(1)} %convolution_bitcast_fusion.1) | data formatting | bytes 4194304
  20.0 2.9 %copy.55 = f32[512,8,128]{0,2,1:T(8,128)} copy(f32[512,8,128]{2,1,0:T(8,128)} %bitcast.68) | data formatting | bytes 4194304 | tf_op jit(solution)/shard_map/reshape | solution.py:13
  22.9 2.2 %reduce_sum.72 = f32[512,8]{1,0:T(8,128)S(1)} reduce(f32[512,8,128]{2,1,0:T(8,128)} %bitcast.69, f32[]{:T(128)} %constant.11.clone.1), dimensions={2}, to_apply=%region_0.0 | reduce | flops 520192 | bytes 2113540 | tf_op jit(solution)/shard_map/reduce_sum | solution.py:14
  25.1 0.1 copy.56
  25.2 0.1 copy.54
  26.0 4.1 %fusion.8 = bf16[512,1024]{1,0:T(8,128)(2,1)} fusion(bf16[512,1024]{1,0:T(8,128)(2,1)} %param.10, bf16[1024,1024]{1,0:T(8,128)(2,1)} %param.13, bf16[512]{0:T(512)(128)(2,1)S(1)} %get-tuple-element.14), kind=kOutput, calls=%fused_computation.25 | convolution fusion | flops 1074790400 | bytes 4195328 | tf_op jit(solution)/shard_map/dot_general | solution.py:48
  30.2 1.5 copy.69
  31.7 0.0 copy-start.5
  31.7 2.0 %multiply_reduce_fusion = f32[512,8]{0,1:T(8,128)S(1)} fusion(f32[512,8,128]{0,2,1:T(8,128)} %copy.57, f32[512,8]{0,1:T(8,128)S(1)} %broadcast_multiply_fusion.4), kind=kLoop, calls=%fused_computation.17 | loop fusion | flops 1568768 | bytes 2129920 | tf_op jit(solution)/shard_map/reduce_sum | solution.py:15
  33.7 0.2 copy-done.3
  33.9 0.3 multiply_reduce_fusion.1
  34.2 1.3 fusion.9
  35.5 0.0 copy-done.1
  35.6 2.0 %fusion.18 = f32[8,128,128]{2,1,0:T(8,128)} fusion(f32[512,8,128]{0,2,1:T(8,128)S(1)} %copy-done.3, f32[8,128]{1,0:T(8,128)S(1)} %bitcast.83, f32[8,128]{1,0:T(8,128)S(1)} %bitcast.75, f32[512,8]{0,1:T(8,128)S(1)} %get-tuple-element.16, f32[512,8]{0,1:T(8,128)S(1)} %broadcast_multiply_fusion.5, f32[512]{0:T(512)S(1)} %get-tuple-element.13, ...), kind=kOutput, calls=%fused_computation.46 | convolution fusion | flops 140509184 | bytes 4802560 | tf_op jit(solution)/shard_map/nhi,nhj->hij/dot_general | solution.py:45
  37.5 0.0 all-reduce.3.cloned.1.call-update
  37.6 35.9 %psum.22 = f32[]{:T(128)} all-reduce(f32[]{:T(128)S(6)} %convert_element_type.64), channel_id=1, replica_groups=mesh['group'=2,'dx'=16] {'dx'}, use_global_device_ids=true, to_apply=%region_5.0 | all-reduce | flops 1 | bytes 8 | tf_op jit(solution)/shard_map/psum | solution.py:34
  73.5 60.4 %all-reduce.3.cloned.1.call-done = (f32[8,128,128]{2,1,0:T(8,128)}, f32[8,128,128]{2,1,0:T(8,128)}) async-done(((f32[8,128,128]{2,1,0:T(8,128)}, f32[8,128,128]{2,1,0:T(8,128)}), (f32[8,128,128]{2,1,0:T(8,128)}, f32[8,128,128]{2,1,0:T(8,128)})) %all-reduce.3.cloned.1.call-update) | async-done | bytes 1048592 | tf_op jit(solution)/shard_map/psum | solution.py:47
  133.9 4.8 %bitcast_reduce_fusion = (f32[512,8]{0,1:T(8,128)S(1)}, f32[512,8]{0,1:T(8,128)S(1)}, f32[8,128,512]{2,1,0:T(8,128)S(1)}) fusion(f32[8,128]{1,0:T(8,128)S(1)} %bitcast.80, f32[512,8]{0,1:T(8,128)S(1)} %get-tuple-element.15, f32[512,8,128]{0,2,1:T(8,128)} %copy.57, f32[512,8]{0,1:T(8,128)S(1)} %broadcast_multiply_fusion.4, f32[512,8,128]{0,2,1:T(8,128)} %copy.55, ...), kind=kOutput, calls=%fused_computation.2 | convolution fusion | flops 140763136 | bytes 6928388 | tf_op jit(solution)/shard_map/nhi,hij->nhj/dot_general | solution.py:60
  138.7 1.7 %bitcast_reduce_fusion.1 = (f32[512,8]{0,1:T(8,128)S(1)}, f32[512,8]{0,1:T(8,128)S(1)}, f32[8,128,512]{2,1,0:T(8,128)S(1)}) fusion(f32[8,128]{1,0:T(8,128)S(1)} %bitcast.77, f32[512,8]{0,1:T(8,128)S(1)} %get-tuple-element.16, f32[512,8,128]{0,2,1:T(8,128)S(1)} %copy-done.4, f32[512,8]{0,1:T(8,128)S(1)} %broadcast_multiply_fusion.5, ...), kind=kOutput, calls=%fused_computation.9 | convolution fusion | flops 140763136 | bytes 6928388 | tf_op jit(solution)/shard_map/nhj,hij->nhi/dot_general | solution.py:59
  140.5 0.8 fusion.6
  141.3 1.3 fusion.21
  142.6 1.3 multiply_convert_fusion
  143.9 0.3 copy-done.9
  144.2 1.3 fusion.20
  145.5 0.8 fusion.2
  146.3 0.8 copy-done.10
  147.1 2.3 %add_convert_fusion = bf16[512,1024]{1,0:T(8,128)(2,1)} fusion(f32[512,1024]{1,0:T(8,128)S(1)} %fusion.20, f32[512,1024]{1,0:T(8,128)S(1)} %fusion.21, bf16[512,1024]{0,1:T(8,128)(2,1)S(1)} %bitcast.73, bf16[1024,1024]{1,0:T(8,128)(2,1)S(1)} %copy-done.10), kind=kOutput, calls=%fused_computation.14 | convolution fusion | flops 1075314688 | bytes 8388608 | tf_op jit(solution)/shard_map/dot_general | solution.py:65
  (36 shorter events, 0.1 us)
Async XLA Ops:
  6.5 10.4 %copy-start = (bf16[1024,1024]{1,0:T(8,128)(2,1)S(1)}, bf16[1024,1024]{1,0:T(8,128)(2,1)}, u32[]{:S(2)}) copy-start(bf16[1024,1024]{1,0:T(8,128)(2,1)} %param.14) | copy-start | bytes 6291460
  6.5 127.3 %all-reduce.3.cloned.1.call-start = ((), (), s32[]{:S(2)}) async-start(), calls=%async_computation | async-start | bytes 2097152 | tf_op jit(solution)/shard_map/psum | solution.py:47
  14.6 2.3 %copy-start.11 = (bf16[512,1024]{1,0:T(8,128)(2,1)S(1)}, bf16[512,1024]{1,0:T(8,128)(2,1)}, u32[]{:S(2)}) copy-start(bf16[512,1024]{1,0:T(8,128)(2,1)} %param.10) | copy-start | bytes 3145732
  31.7 2.2 %copy-start.3 = (f32[512,8,128]{0,2,1:T(8,128)S(1)}, f32[512,8,128]{0,2,1:T(8,128)}, u32[]{:S(2)}) copy-start(f32[512,8,128]{0,2,1:T(8,128)} %copy.55) | copy-start | bytes 6291460
  31.7 2.6 %copy-start.5 = (bf16[512,1024]{1,0:T(8,128)(2,1)S(1)}, bf16[512,1024]{1,0:T(8,128)(2,1)}, u32[]{:S(2)}) copy-start(bf16[512,1024]{1,0:T(8,128)(2,1)} %param.11) | copy-start | bytes 3145732
  33.9 1.7 %copy-start.1 = (f32[512,8,128]{0,2,1:T(8,128)S(1)}, f32[512,8,128]{0,2,1:T(8,128)}, u32[]{:S(2)}) copy-start(f32[512,8,128]{0,2,1:T(8,128)} %copy.57) | copy-start | bytes 6291460
  33.9 1.7 %copy-start.7 = (f32[1024]{0:T(1024)S(1)}, f32[1024]{0:T(1024)}, u32[]{:S(2)}) copy-start(f32[1024]{0:T(1024)} %param.16) | copy-start | bytes 12292
  33.9 1.7 %copy-start.8 = (f32[1024]{0:T(1024)S(1)}, f32[1024]{0:T(1024)}, u32[]{:S(2)}) copy-start(f32[1024]{0:T(1024)} %param.18) | copy-start | bytes 12292
  33.9 1.7 %copy-start.14 = (f32[1024]{0:T(1024)S(1)}, f32[1024]{0:T(1024)}, u32[]{:S(2)}) copy-start(f32[1024]{0:T(1024)} %param.17) | copy-start | bytes 12292
  33.9 1.7 %copy-start.15 = (f32[1024]{0:T(1024)S(1)}, f32[1024]{0:T(1024)}, u32[]{:S(2)}) copy-start(f32[1024]{0:T(1024)} %param.19) | copy-start | bytes 12292
  133.9 4.8 %copy-start.2 = (f32[512,8,128]{0,2,1:T(8,128)S(1)}, f32[512,8,128]{0,2,1:T(8,128)}, u32[]{:S(2)}) copy-start(f32[512,8,128]{0,2,1:T(8,128)} %copy.57) | copy-start | bytes 6291460
  133.9 4.8 %copy-start.4 = (f32[512,8,128]{0,2,1:T(8,128)S(1)}, f32[512,8,128]{0,2,1:T(8,128)}, u32[]{:S(2)}) copy-start(f32[512,8,128]{0,2,1:T(8,128)} %copy.55) | copy-start | bytes 6291460
  133.9 4.8 %copy-start.13 = (f32[8,128,128]{2,1,0:T(8,128)S(1)}, f32[8,128,128]{2,1,0:T(8,128)}, u32[]{:S(2)}) copy-start(f32[8,128,128]{2,1,0:T(8,128)} %get-tuple-element.10) | copy-start | bytes 1572868
  141.3 1.4 copy-start.6
  141.3 1.4 copy-start.12
  142.6 1.6 %copy-start.9 = (bf16[1024,1024]{1,0:T(8,128)(2,1)S(1)}, bf16[1024,1024]{1,0:T(8,128)(2,1)}, u32[]{:S(2)}) copy-start(bf16[1024,1024]{1,0:T(8,128)(2,1)} %param.13) | copy-start | bytes 6291460
  145.5 1.6 %copy-start.10 = (bf16[1024,1024]{1,0:T(8,128)(2,1)S(1)}, bf16[1024,1024]{1,0:T(8,128)(2,1)}, u32[]{:S(2)}) copy-start(bf16[1024,1024]{1,0:T(8,128)(2,1)} %param.15) | copy-start | bytes 6291460
Sparse Core Ops, SparseCore 0:
  37.7 96.1 all-reduce.2
where the time goes:
time: 157 us; the launch traced here: 156 us
  waiting for transfers between devices  60.4 us (38%)
  blocking collectives  35.9 us (23%)
  matrix products  24.6 us (16%)
  between operations  14.3 us (9%)
  local copies, waits for them, and re-layouts  12.5 us (8%)
  other arithmetic  8.47 us (5%)
    psum x1, waiting for transfers between devices, body(): kv_sum = lax.psum(kv_local, 'dx')  60.4 us
    psum x1, blocking collectives, body(): total = lax.psum(own_count, 'dx')  35.9 us
    reshape x2, local copies, waits for them, and re-layouts, head_norm(): grouped = raw.reshape(raw.shape[0], heads, -1)  5.92 us
    unnamed x34, local copies, waits for them, and re-layouts  4.87 us
    dot_general x1, matrix products, body(): jnp.einsum('nhi,hij->nhj', keys, dgram, preferred_element_type=jnp.float32)  4.81 us
    reduce_sum x2, other arithmetic, head_norm(): center = grouped - jnp.mean(grouped, axis=2, keepdims=True)  4.51 us
    dot_general x1, matrix products, body(): jnp.dot(points, w_query, preferred_element_type=jnp.float32)  4.15 us
    dot_general x1, matrix products, body(): jnp.dot(points, w_value, preferred_element_type=jnp.float32)  3.3 us
  transfers between devices with their start and end apart: 1, of which 1 were waited for; matrix products, arithmetic and copies ran while one was open for 0% of the time, Pallas kernels for 0%

commit v1 on v0

v1 whole, which is shorter than its diff:
```python
import functools

import jax
import jax.numpy as jnp
from jax import lax
from jax.experimental import pallas as pl
from jax.experimental.pallas import tpu as pltpu
from jax.sharding import PartitionSpec as P

HEADS = 8
EPS = 1e-05
MESH = pl.DeviceIdType.MESH
F32 = jnp.float32
BF16 = jnp.bfloat16
NT = (((1,), (1,)), ((), ()))
TN = (((0,), (0,)), ((), ()))
NN = (((1,), (0,)), ((), ()))


def mm(a, b, dims):
    return lax.dot_general(a, b, dims, preferred_element_type=F32)


def kernel(
    n,
    counts,
    points_hbm,
    cot_hbm,
    wq_hbm,
    wk_hbm,
    wv_hbm,
    gain_k,
    bias_k,
    gain_v,
    bias_v,
    out_hbm,
    points,
    cot,
    wq,
    wk,
    wv,
    khat,
    vhat,
    kinv,
    vinv,
    keys,
    values,
    dq,
    dk,
    dv,
    acc,
    out,
    loc,
    r1,
    p1,
    r2,
    p2,
    r3,
    p3,
    full,
    cnt,
    cr,
    load_sem,
    store_sem,
    send_sem,
    recv_sem,
    csend_sem,
    crecv_sem,
):
    rows, width = points.shape
    hd = width // HEADS
    pair = 2 * hd
    npair = HEADS // 2
    grows = HEADS * hd
    far = n // 4
    piece = grows // n

    me = lax.axis_index("dx")
    core = lax.rem(me, 2)
    mid = lax.rem(me // 2, 2)
    hi = me // 4
    core_peer = me + 1 - 2 * core
    mid_peer = me + 2 - 4 * mid
    low = lax.rem(me, 4)
    far_peers = [lax.rem(hi + d, far) * 4 + low for d in range(1, far)]

    def load(src, dst, i):
        return pltpu.make_async_copy(src, dst, load_sem.at[i])

    loads = [
        load(points_hbm, points, 0),
        load(wq_hbm, wq, 1),
        load(cot_hbm, cot, 2),
        load(wk_hbm, wk, 3),
        load(wv_hbm, wv, 4),
    ]
    for c in loads:
        c.start()

    barrier = pltpu.get_barrier_semaphore()
    for p in [core_peer, mid_peer] + far_peers:
        pl.semaphore_signal(barrier, inc=1, device_id={"dx": p}, device_id_type=MESH)

    own_count = counts[0]

    def live(cols):
        return lax.broadcasted_iota(jnp.int32, (rows, cols), 0) < own_count

    def rcopy(src, dst, sems, rsems, k, peer):
        return pltpu.make_async_remote_copy(
            src_ref=src,
            dst_ref=dst,
            send_sem=sems.at[k],
            recv_sem=rsems.at[k],
            device_id={"dx": peer},
            device_id_type=MESH,
        )

    half, quarter = grows // 2, grows // 4

    def block(i, size):
        return pl.ds(pl.multiple_of(i * size, size), size)

    sent = []

    def go(copies):
        for c in copies:
            c.start()
        sent.extend(copies)

    def arrive(copies):
        for c in copies:
            c.wait_recv()

    def scatter1(c):
        x = [rcopy(loc.at[c, block(1 - core, half)], r1.at[c], send_sem.at[c], recv_sem.at[c], 0, core_peer)]
        if c == 0:
            x.append(rcopy(cnt.at[0], cr.at[0], csend_sem, crecv_sem, 0, core_peer))
        go(x)
        return x

    def scatter2(c, before):
        arrive(before)
        p1[c] = loc[c, block(core, half), :] + r1[c]
        x = [rcopy(p1.at[c, block(1 - mid, quarter)], r2.at[c], send_sem.at[c], recv_sem.at[c], 1, mid_peer)]
        if c == 0:
            cnt[1] = cnt[0] + cr[0]
            x.append(rcopy(cnt.at[1], cr.at[1], csend_sem, crecv_sem, 1, mid_peer))
        go(x)
        return x

    def scatter3(c, before):
        arrive(before)
        p2[c] = p1[c, block(mid, quarter), :] + r2[c]
        x = []
        if c == 0:
            cnt[2] = cnt[1] + cr[1]
        for d in range(1, far):
            to = lax.rem(hi + d, far)
            x.append(
                rcopy(
                    p2.at[c, block(to, piece)],
                    r3.at[c, d],
                    send_sem.at[c],
                    recv_sem.at[c],
                    1 + d,
                    far_peers[d - 1],
                )
            )
            if c == 0:
                x.append(rcopy(cnt.at[2], cr.at[1 + d], csend_sem, crecv_sem, 1 + d, far_peers[d - 1]))
        go(x)
        return x

    base = far + 1
    own = core * half + mid * quarter + hi * piece

    def gather1(c, before):
        arrive(before)
        total = p2[c, block(hi, piece), :]
        for d in range(1, far):
            total = total + r3[c, d]
        if c == 0:
            people = cnt[2]
            for d in range(1, far):
                people = people + cr[1 + d]
            cnt[3] = people
        total = total / cnt[3, 0:1, :]
        where = pl.ds(pl.multiple_of(own, piece), piece)
        full[c, where, :] = total
        x = []
        for d in range(1, far):
            x.append(
                rcopy(
                    full.at[c, where],
                    full.at[c, where],
                    send_sem.at[c],
                    recv_sem.at[c],
                    base + d - 1,
                    far_peers[d - 1],
                )
            )
        go(x)
        return x

    def gather2(c, before):
        arrive(before)
        where = pl.ds(pl.multiple_of(core * half + mid * quarter, quarter), quarter)
        x = [rcopy(full.at[c, where], full.at[c, where], send_sem.at[c], recv_sem.at[c], base + far - 1, mid_peer)]
        go(x)
        return x

    def gather3(c, before):
        arrive(before)
        where = block(core, half)
        x = [rcopy(full.at[c, where], full.at[c, where], send_sem.at[c], recv_sem.at[c], base + far, core_peer)]
        go(x)
        return x

    cnt[0] = jnp.broadcast_to(own_count.astype(F32), cnt.shape[1:])
    loads[0].wait()
    loads[1].wait()
    loads[2].wait()

    @pl.loop(0, npair)
    def _(hp):
        cols = block(hp, pair)
        q = mm(points[...], wq[:, cols], NN)
        q = jnp.where(live(pair), q, 0.0).astype(BF16)
        g = mm(q, cot[:, cols], TN)
        r = pl.multiple_of(hp * pair, pair)
        loc[0, pl.ds(r, hd), :] = g[:hd, :hd]
        loc[0, pl.ds(r + hd, hd), :] = g[hd:, hd:]

    pl.semaphore_wait(barrier, far + 1)
    stage = scatter1(0)
    loads[3].wait()
    loads[4].wait()

    def norm(raw, gain, bias, hat_ref, inv_ref, dst, c0):
        for j in range(2):
            x = raw[:, j * hd : (j + 1) * hd]
            cs = slice(c0 + j * hd, c0 + (j + 1) * hd)
            center = x - jnp.mean(x, axis=1, keepdims=True)
            inv = lax.rsqrt(jnp.mean(center * center, axis=1, keepdims=True) + EPS)
            hat = center * inv
            hat_ref[:, cs] = hat
            inv_ref[:, cs] = jnp.broadcast_to(inv, hat.shape)
            y = hat * gain[:, cs] + bias[:, cs]
            dst[:, cs] = jnp.where(live(hd), y, 0.0).astype(BF16)

    def forward(hp):
        c0 = hp * pair
        cs = slice(c0, c0 + pair)
        norm(mm(points[...], wk[:, cs], NN), gain_k, bias_k, khat, kinv, keys, c0)
        norm(mm(points[...], wv[:, cs], NN), gain_v, bias_v, vhat, vinv, values, c0)
        g = mm(keys[:, cs], values[:, cs], TN)
        loc[1, c0 : c0 + hd, :] = g[:hd, :hd]
        loc[1, c0 + hd : c0 + pair, :] = g[hd:, hd:]

    steps = [scatter2, scatter3, gather1, gather2]
    for hp in range(npair):
        forward(hp)
        if hp < len(steps):
            stage = steps[hp](0, stage)

    kv = scatter1(1)
    stage = gather3(0, stage)
    kv = scatter2(1, kv)
    arrive(stage)

    def back(grad, gain, hat_ref, inv_ref, dst, cs):
        g = grad * gain[:, cs]
        hat = hat_ref[:, cs]
        inner = g - jnp.mean(g, axis=1, keepdims=True)
        inner = inner - hat * jnp.mean(g * hat, axis=1, keepdims=True)
        dst[:, cs] = (inv_ref[:, cs] * inner).astype(BF16)

    def backward(hp):
        for h in (2 * hp, 2 * hp + 1):
            cs = slice(h * hd, (h + 1) * hd)
            d = full[0, cs, :].astype(BF16)
            back(mm(values[:, cs], d, NT), gain_k, khat, kinv, dk, cs)
            back(mm(keys[:, cs], d, NN), gain_v, vhat, vinv, dv, cs)

    for hp in range(npair):
        backward(hp)
        if hp == 0:
            kv = scatter3(1, kv)
        if hp == 2:
            kv = gather1(1, kv)

    def tail(i):
        rs = block(i, pair)
        acc[:, rs] = mm(dk[...], wk[rs, :], NT) + mm(dv[...], wv[rs, :], NT)

    for i in range(npair):
        tail(i)
        if i == 0:
            kv = gather2(1, kv)
        if i == 2:
            kv = gather3(1, kv)
    arrive(kv)

    for h in range(HEADS):
        cs = slice(h * hd, (h + 1) * hd)
        g = full[1, cs, :].astype(BF16)
        dq[:, cs] = jnp.where(live(hd), mm(cot[:, cs], g, NT), 0.0).astype(BF16)

    writes = []
    for i in range(npair):
        cs = slice(i * pair, (i + 1) * pair)
        out[:, cs] = (acc[:, cs] + mm(dq[...], wq[cs, :], NT)).astype(BF16)
        w = pltpu.make_async_copy(out.at[:, cs], out_hbm.at[:, cs], store_sem.at[i])
        w.start()
        writes.append(w)
    for c in sent:
        c.wait_send()
    for w in writes:
        w.wait()


def body(n, points, cotangent, counts, w_query, w_key, w_value, gain_key, bias_key, gain_value, bias_value):
    rows, width = points.shape
    hd = width // HEADS
    grows = HEADS * hd
    far = n // 4
    piece = grows // n
    ncopies = 2 * (far + 1)
    anyspec = pl.BlockSpec(memory_space=pl.ANY)
    vspec = pl.BlockSpec(memory_space=pltpu.VMEM)

    def v(shape, dtype):
        return pltpu.VMEM(shape, dtype)

    return pl.pallas_call(
        functools.partial(kernel, n),
        out_shape=jax.ShapeDtypeStruct((rows, width), BF16),
        in_specs=[pl.BlockSpec(memory_space=pltpu.SMEM)] + [anyspec] * 5 + [vspec] * 4,
        out_specs=anyspec,
        scratch_shapes=[
            v((rows, width), BF16),
            v((rows, width), BF16),
            v((width, width), BF16),
            v((width, width), BF16),
            v((width, width), BF16),
            v((rows, width), F32),
            v((rows, width), F32),
            v((rows, width), F32),
            v((rows, width), F32),
            v((rows, width), BF16),
            v((rows, width), BF16),
            v((rows, width), BF16),
            v((rows, width), BF16),
            v((rows, width), BF16),
            v((rows, width), F32),
            v((rows, width), BF16),
            v((2, grows, hd), F32),
            v((2, grows // 2, hd), F32),
            v((2, grows // 2, hd), F32),
            v((2, grows // 4, hd), F32),
            v((2, grows // 4, hd), F32),
            v((2, far, piece, hd), F32),
            v((2, piece, hd), F32),
            v((2, grows, hd), F32),
            v((4, 8, hd), F32),
            v((far + 1, 8, hd), F32),
            pltpu.SemaphoreType.DMA((5,)),
            pltpu.SemaphoreType.DMA((HEADS // 2,)),
            pltpu.SemaphoreType.DMA((2, ncopies)),
            pltpu.SemaphoreType.DMA((2, ncopies)),
            pltpu.SemaphoreType.DMA((far + 1,)),
            pltpu.SemaphoreType.DMA((far + 1,)),
        ],
        compiler_params=pltpu.CompilerParams(
            collective_id=0, has_side_effects=True, vmem_limit_bytes=52 * 2**20
        ),
        cost_estimate=pl.CostEstimate(
            flops=12 * rows * width * width, bytes_accessed=12 * 2**20, transcendentals=0
        ),
    )(
        counts,
        points,
        cotangent,
        w_query,
        w_key,
        w_value,
        gain_key.reshape(1, -1),
        bias_key.reshape(1, -1),
        gain_value.reshape(1, -1),
        bias_value.reshape(1, -1),
    )


def solution(mesh):
    split = P(("group", "dx"), None)
    placed = (split, split, P(("group", "dx")), P(), P(), P(), P(), P(), P(), P())
    return jax.shard_map(
        functools.partial(body, mesh.shape["dx"]),
        mesh=mesh,
        in_specs=placed,
        out_specs=split,
        check_vma=False,
    )
```

time: 157 us -> 53.1 us (0.34)
  waiting for transfers between devices: 60.4 us -> 0 us
  Pallas kernels: 0 us -> 48.4 us
  blocking collectives: 35.9 us -> 0 us
  matrix products: 24.6 us -> 0 us
  between operations: 14.3 us -> 0.67 us
  local copies, waits for them, and re-layouts: 12.5 us -> 3.71 us
  other arithmetic: 8.47 us -> 0 us
    psum x1 -> x0, waiting for transfers between devices: 60.4 us -> none  [body(): kv_sum = lax.psum(kv_local, 'dx')]
    pallas_call x0 -> x1, Pallas kernels: none -> 48.4 us  [body(): pl.pallas_call(functools.partial(kernel, n), out_shape=jax.ShapeDtypeStru...]
    psum x1 -> x0, blocking collectives: 35.9 us -> none  [body(): total = lax.psum(own_count, 'dx')]
    dot_general x11 -> x0, matrix products: 24.6 us -> none  [the longest x1 4.81 us: body(): jnp.einsum('nhi,hij->nhj', keys, dgram, preferred_element_type=jnp.float32)]
    reshape x3 -> x0, local copies, waits for them, and re-layouts: 7.41 us -> none  [the longest x2 5.92 us: head_norm(): grouped = raw.reshape(raw.shape[0], heads, -1)]
    reduce_sum x4 -> x0, other arithmetic: 6.85 us -> none  [the longest x2 4.51 us: head_norm(): center = grouped - jnp.mean(grouped, axis=2, keepdims=True)]
    convert_element_type x3 -> x0, other arithmetic: 1.58 us -> none  [the longest x2 1.57 us: norm_back(): return (inverse * inner).reshape(grad.shape[0], -1).astype(jnp.bfloat16)]
    unnamed x34 -> x9, local copies, waits for them, and re-layouts: 4.87 us -> 3.71 us
  transfers between devices with their start and end apart: 1 -> 0, of which waited for: 1 -> 0; matrix products, arithmetic and copies ran while one was open for 0% -> 0% of each run, Pallas kernels for 0% -> 0%
where the time goes in v1:
time: 53.1 us; the launch traced here: 52.8 us
  Pallas kernels  48.4 us (91%)
  local copies, waits for them, and re-layouts  3.71 us (7%)
  between operations  0.67 us (1%)
    pallas_call x1, Pallas kernels, body(): pl.pallas_call(functools.partial(kernel, n), out_shape=jax.ShapeDtypeStru...  48.4 us
    unnamed x9, local copies, waits for them, and re-layouts  3.71 us

profile of v1, /device:TPU:0, one launch (start us, length us, event | category | flops | bytes accessed | tf_op | source)
XLA Modules:
  0.0 52.8 jit_solution(11807531854545785973)
XLA Ops:
  0.7 0.0 copy-start
  0.7 0.7 %copy-done = f32[1024]{0:T(1024)S(1)} copy-done((f32[1024]{0:T(1024)S(1)}, f32[1024]{0:T(1024)}, u32[]{:S(2)}) %copy-start) | copy-done | bytes 4120
  1.3 0.0 copy-start.1
  1.3 0.7 %copy-done.1 = f32[1024]{0:T(1024)S(1)} copy-done((f32[1024]{0:T(1024)S(1)}, f32[1024]{0:T(1024)}, u32[]{:S(2)}) %copy-start.1) | copy-done | bytes 4120
  2.0 0.0 copy-start.2
  2.0 0.7 %copy-done.2 = f32[1024]{0:T(1024)S(1)} copy-done((f32[1024]{0:T(1024)S(1)}, f32[1024]{0:T(1024)}, u32[]{:S(2)}) %copy-start.2) | copy-done | bytes 4120
  2.7 0.0 copy-start.3
  2.7 0.7 %copy-done.3 = f32[1024]{0:T(1024)S(1)} copy-done((f32[1024]{0:T(1024)S(1)}, f32[1024]{0:T(1024)}, u32[]{:S(2)}) %copy-start.3) | copy-done | bytes 4120
  3.4 48.4 %shard_map.100 = bf16[512,1024]{1,0:T(8,128)(2,1)S(1)} custom-call(s32[1]{0:T(128)S(6)} %copy.12.counts, bf16[512,1024]{1,0:T(8,128)(2,1)} %points_hbm.1, bf16[512,1024]{1,0:T(8,128)(2,1)} %cot_hbm.1, bf16[1024,1024]{1,0:T(8,128)(2,1)} %wq_hbm.1, bf16[1024,1024]{1,0:T(8,128)(2,1)} %wk_hbm.1, bf16[1024,1024]{1,0:T(8,128)(2,1)} %wv_hbm.1, ...), custom_call_target="tpu_custom_call" | custom-call | flops 6442450944 | bytes 12582912 | tf_op jit(solution)/shard_map/pallas_call | solution.py:336
  51.8 1.0 %copy.13 = bf16[512,1024]{1,0:T(8,128)(2,1)} copy(bf16[512,1024]{1,0:T(8,128)(2,1)S(1)} %shard_map.100) | data formatting | bytes 2097152
Async XLA Ops:
  0.7 0.7 %copy-start = (f32[1024]{0:T(1024)S(1)}, f32[1024]{0:T(1024)}, u32[]{:S(2)}) copy-start(f32[1024]{0:T(1024)} %param.16) | copy-start | bytes 12292
  1.3 0.7 %copy-start.1 = (f32[1024]{0:T(1024)S(1)}, f32[1024]{0:T(1024)}, u32[]{:S(2)}) copy-start(f32[1024]{0:T(1024)} %param.17) | copy-start | bytes 12292
  2.0 0.7 %copy-start.2 = (f32[1024]{0:T(1024)S(1)}, f32[1024]{0:T(1024)}, u32[]{:S(2)}) copy-start(f32[1024]{0:T(1024)} %param.18) | copy-start | bytes 12292
  2.7 0.7 %copy-start.3 = (f32[1024]{0:T(1024)S(1)}, f32[1024]{0:T(1024)}, u32[]{:S(2)}) copy-start(f32[1024]{0:T(1024)} %param.19) | copy-start | bytes 12292

commit v2 on v1

v2 whole, which is shorter than its diff:
```python
import functools

import jax
import jax.numpy as jnp
from jax import lax
from jax.experimental import pallas as pl
from jax.experimental.pallas import tpu as pltpu
from jax.sharding import PartitionSpec as P

HEADS = 8
EPS = 1e-05
MESH = pl.DeviceIdType.MESH
F32 = jnp.float32
BF16 = jnp.bfloat16
NT = (((1,), (1,)), ((), ()))
TN = (((0,), (0,)), ((), ()))
NN = (((1,), (0,)), ((), ()))


def mm(a, b, dims):
    return lax.dot_general(a, b, dims, preferred_element_type=F32)


def kernel(
    n,
    counts,
    points_hbm,
    cot_hbm,
    wq_hbm,
    wk_hbm,
    wv_hbm,
    gk_hbm,
    bk_hbm,
    gv_hbm,
    bv_hbm,
    out,
    points,
    cot,
    wq,
    wk,
    wv,
    khat,
    vhat,
    kinv,
    vinv,
    keys,
    values,
    dq,
    dk,
    dv,
    gain_k,
    bias_k,
    gain_v,
    bias_v,
    acc,
    loc,
    r1,
    p1,
    r3,
    full,
    cnt,
    load_sem,
    send_sem,
    recv_sem,
    csend_sem,
    crecv_sem,
):
    rows, width = points.shape
    hd = width // HEADS
    pair = 2 * hd
    npair = HEADS // 2
    grows = HEADS * hd
    chips = n // 2
    piece = grows // n

    me = lax.axis_index("dx")
    core = lax.rem(me, 2)
    chip = me // 2
    core_peer = me + 1 - 2 * core
    chip_peers = [lax.rem(chip + d, chips) * 2 + core for d in range(1, chips)]

    def load(src, dst, i):
        return pltpu.make_async_copy(src, dst, load_sem.at[i])

    loads = [
        load(points_hbm, points, 0),
        load(wq_hbm, wq, 1),
        load(cot_hbm, cot, 2),
        load(wk_hbm, wk, 3),
        load(wv_hbm, wv, 4),
        load(gk_hbm, gain_k, 5),
        load(bk_hbm, bias_k, 6),
        load(gv_hbm, gain_v, 7),
        load(bv_hbm, bias_v, 8),
    ]
    for c in loads:
        c.start()

    barrier = pltpu.get_barrier_semaphore()
    for p in [core_peer] + chip_peers:
        pl.semaphore_signal(barrier, inc=1, device_id={"dx": p}, device_id_type=MESH)

    own_count = counts[0]

    def live(cols):
        return lax.broadcasted_iota(jnp.int32, (rows, cols), 0) < own_count

    def rcopy(src, dst, sems, rsems, k, peer):
        return pltpu.make_async_remote_copy(
            src_ref=src,
            dst_ref=dst,
            send_sem=sems.at[k],
            recv_sem=rsems.at[k],
            device_id={"dx": peer},
            device_id_type=MESH,
        )

    half = grows // 2

    def block(i, size):
        return pl.ds(pl.multiple_of(i * size, size), size)

    sent = []

    def go(copies):
        for c in copies:
            c.start()
        sent.extend(copies)

    def arrive(copies):
        for c in copies:
            c.wait_recv()

    def core_scatter(c):
        x = [rcopy(loc.at[c, block(1 - core, half)], r1.at[c], send_sem.at[c], recv_sem.at[c], 0, core_peer)]
        if c == 0:
            x.append(rcopy(cnt.at[0], cnt.at[1], csend_sem, crecv_sem, 0, core_peer))
        go(x)
        return x

    def chip_scatter(c, before):
        arrive(before)
        for j in range(chips):
            mine = pl.ds(pl.multiple_of(core * half + j * piece, piece), piece)
            p1[c, j, 0:piece, :] = loc[c, mine, :] + r1[c, j * piece : (j + 1) * piece, :]
        if c == 0:
            people = cnt[0] + cnt[1]
            for j in range(chips):
                p1[c, j, piece:, :] = people
        size = piece + 8 if c == 0 else piece
        x = []
        for d in range(1, chips):
            x.append(
                rcopy(
                    p1.at[c, lax.rem(chip + d, chips), pl.ds(0, size)],
                    r3.at[c, d, pl.ds(0, size)],
                    send_sem.at[c],
                    recv_sem.at[c],
                    d,
                    chip_peers[d - 1],
                )
            )
        go(x)
        return x

    def span(j):
        return pl.ds(pl.multiple_of(core * half + j * piece, piece), piece)

    def chip_gather(c, before):
        arrive(before)
        total = p1[c, chip, 0:piece, :]
        for d in range(1, chips):
            total = total + r3[c, d, 0:piece, :]
        if c == 0:
            people = p1[c, chip, piece:, :]
            for d in range(1, chips):
                people = people + r3[c, d, piece:, :]
            cnt[2] = people
        full[c, span(chip), :] = total / cnt[2, 0:1, :]
        x = []
        for d in range(1, chips):
            x.append(
                rcopy(
                    full.at[c, span(chip)],
                    full.at[c, span(chip)],
                    send_sem.at[c],
                    recv_sem.at[c],
                    chips + d,
                    chip_peers[d - 1],
                )
            )
        go(x)
        y = [core_forward(c, 0)]
        go(y)
        return x, y

    def core_forward(c, d):
        rs = span(lax.rem(chip + chips - d, chips))
        return rcopy(full.at[c, rs], full.at[c, rs], send_sem.at[c], recv_sem.at[c], 2 * chips + d, core_peer)

    def core_gather(c, before):
        x, y = before
        for d in range(1, chips):
            x[d - 1].wait_recv()
            f = core_forward(c, d)
            go([f])
            y.append(f)
        return y

    own_pairs = [core * (npair // 2) + i for i in range(npair // 2)]
    peer_pairs = [(1 - core) * (npair // 2) + i for i in range(npair // 2)]

    cnt[0] = jnp.broadcast_to(own_count.astype(F32), cnt.shape[1:])
    loads[0].wait()
    loads[1].wait()
    loads[2].wait()

    def query(hp):
        cols = block(hp, pair)
        q = mm(points[...], wq[:, cols], NN)
        q = jnp.where(live(pair), q, 0.0).astype(BF16)
        g = mm(q, cot[:, cols], TN)
        r = pl.multiple_of(hp * pair, pair)
        loc[0, pl.ds(r, hd), :] = g[:hd, :hd]
        loc[0, pl.ds(r + hd, hd), :] = g[hd:, hd:]

    for hp in peer_pairs:
        query(hp)
    pl.semaphore_wait(barrier, chips)
    qdy = core_scatter(0)
    for hp in own_pairs:
        query(hp)
    for c in loads[3:]:
        c.wait()
    qdy = chip_scatter(0, qdy)

    def norm(raw, gain, bias, hat_ref, inv_ref, dst, c0):
        for j in range(2):
            x = raw[:, j * hd : (j + 1) * hd]
            cs = pl.ds(pl.multiple_of(c0 + j * hd, hd), hd)
            center = x - jnp.mean(x, axis=1, keepdims=True)
            inv = lax.rsqrt(jnp.mean(center * center, axis=1, keepdims=True) + EPS)
            hat = center * inv
            hat_ref[:, cs] = hat
            inv_ref[:, cs] = jnp.broadcast_to(inv, hat.shape)
            y = hat * gain[:, cs] + bias[:, cs]
            dst[:, cs] = jnp.where(live(hd), y, 0.0).astype(BF16)

    def forward(hp):
        c0 = pl.multiple_of(hp * pair, pair)
        cs = pl.ds(c0, pair)
        norm(mm(points[...], wk[:, cs], NN), gain_k, bias_k, khat, kinv, keys, c0)
        norm(mm(points[...], wv[:, cs], NN), gain_v, bias_v, vhat, vinv, values, c0)
        g = mm(keys[:, cs], values[:, cs], TN)
        loc[1, pl.ds(c0, hd), :] = g[:hd, :hd]
        loc[1, pl.ds(pl.multiple_of(c0 + hd, hd), hd), :] = g[hd:, hd:]

    for hp in peer_pairs:
        forward(hp)
    kv = core_scatter(1)
    for hp in own_pairs:
        forward(hp)
    kv = chip_scatter(1, kv)
    qdy = chip_gather(0, qdy)
    kv = chip_gather(1, kv)
    qdy = core_gather(0, qdy)

    def back(grad, gain, hat_ref, inv_ref, dst, cs):
        g = grad * gain[:, cs]
        hat = hat_ref[:, cs]
        inner = g - jnp.mean(g, axis=1, keepdims=True)
        inner = inner - hat * jnp.mean(g * hat, axis=1, keepdims=True)
        dst[:, cs] = (inv_ref[:, cs] * inner).astype(BF16)

    def backward(hp):
        for j in range(2):
            cs = block(2 * hp + j, hd)
            d = full[0, cs, :].astype(BF16)
            back(mm(values[:, cs], d, NT), gain_k, khat, kinv, dk, cs)
            back(mm(keys[:, cs], d, NN), gain_v, vhat, vinv, dv, cs)

    def tail(i):
        rs = slice(i * pair, (i + 1) * pair)
        acc[:, rs] = mm(dk[...], wk[rs, :], NT) + mm(dv[...], wv[rs, :], NT)

    for hp in own_pairs:
        backward(hp)
    arrive(qdy)
    for hp in peer_pairs:
        backward(hp)
    for i in range(npair):
        tail(i)

    def dquery(hp):
        for j in range(2):
            cs = block(2 * hp + j, hd)
            g = full[1, cs, :].astype(BF16)
            dq[:, cs] = jnp.where(live(hd), mm(cot[:, cs], g, NT), 0.0).astype(BF16)

    kv = core_gather(1, kv)
    for hp in own_pairs:
        dquery(hp)
    cs = block(core, width // 2)
    for i in range(npair):
        rs = slice(i * pair, (i + 1) * pair)
        acc[:, rs] += mm(dq[:, cs], wq[rs, cs], NT)
    arrive(kv)
    for hp in peer_pairs:
        dquery(hp)
    cs = block(1 - core, width // 2)
    for i in range(npair):
        rs = slice(i * pair, (i + 1) * pair)
        out[:, rs] = (acc[:, rs] + mm(dq[:, cs], wq[rs, cs], NT)).astype(BF16)
    for c in sent:
        c.wait_send()


def body(n, points, cotangent, counts, w_query, w_key, w_value, gain_key, bias_key, gain_value, bias_value):
    rows, width = points.shape
    hd = width // HEADS
    grows = HEADS * hd
    chips = n // 2
    piece = grows // n
    ncopies = 3 * chips
    anyspec = pl.BlockSpec(memory_space=pl.ANY)
    vspec = pl.BlockSpec(memory_space=pltpu.VMEM)

    def v(shape, dtype):
        return pltpu.VMEM(shape, dtype)

    return pl.pallas_call(
        functools.partial(kernel, n),
        out_shape=jax.ShapeDtypeStruct((rows, width), BF16),
        in_specs=[pl.BlockSpec(memory_space=pltpu.SMEM)] + [anyspec] * 5 + [pl.BlockSpec(memory_space=pltpu.HBM)] * 4,
        out_specs=vspec,
        scratch_shapes=[
            v((rows, width), BF16),
            v((rows, width), BF16),
            v((width, width), BF16),
            v((width, width), BF16),
            v((width, width), BF16),
            v((rows, width), F32),
            v((rows, width), F32),
            v((rows, width), F32),
            v((rows, width), F32),
            v((rows, width), BF16),
            v((rows, width), BF16),
            v((rows, width), BF16),
            v((rows, width), BF16),
            v((rows, width), BF16),
            v((1, width), F32),
            v((1, width), F32),
            v((1, width), F32),
            v((1, width), F32),
            v((rows, width), F32),
            v((2, grows, hd), F32),
            v((2, grows // 2, hd), F32),
            v((2, chips, piece + 8, hd), F32),
            v((2, chips, piece + 8, hd), F32),
            v((2, grows, hd), F32),
            v((3, 8, hd), F32),
            pltpu.SemaphoreType.DMA((9,)),
            pltpu.SemaphoreType.DMA((2, ncopies)),
            pltpu.SemaphoreType.DMA((2, ncopies)),
            pltpu.SemaphoreType.DMA((1,)),
            pltpu.SemaphoreType.DMA((1,)),
        ],
        compiler_params=pltpu.CompilerParams(
            collective_id=0, has_side_effects=True, vmem_limit_bytes=63 * 2**20
        ),
        cost_estimate=pl.CostEstimate(
            flops=12 * rows * width * width, bytes_accessed=12 * 2**20, transcendentals=0
        ),
    )(
        counts,
        points,
        cotangent,
        w_query,
        w_key,
        w_value,
        gain_key.reshape(1, -1),
        bias_key.reshape(1, -1),
        gain_value.reshape(1, -1),
        bias_value.reshape(1, -1),
    )


def solution(mesh):
    split = P(("group", "dx"), None)
    placed = (split, split, P(("group", "dx")), P(), P(), P(), P(), P(), P(), P())
    return jax.shard_map(
        functools.partial(body, mesh.shape["dx"]),
        mesh=mesh,
        in_specs=placed,
        out_specs=split,
        check_vma=False,
    )
```

time: 53.1 us -> 40.9 us (0.77)
  Pallas kernels: 48.4 us -> 37.8 us
  local copies, waits for them, and re-layouts: 3.71 us -> 2.26 us
    pallas_call x1, Pallas kernels: 48.4 us -> 37.8 us  [body(): pl.pallas_call(functools.partial(kernel, n), out_shape=jax.ShapeDtypeStru...]
    unnamed x9 -> x1, local copies, waits for them, and re-layouts: 3.71 us -> 2.26 us
where the time goes in v2:
time: 40.9 us; the launch traced here: 40.7 us
  Pallas kernels  37.8 us (92%)
  local copies, waits for them, and re-layouts  2.26 us (6%)
  between operations  0.66 us (2%)
    pallas_call x1, Pallas kernels, body(): pl.pallas_call(functools.partial(kernel, n), out_shape=jax.ShapeDtypeStru...  37.8 us
    unnamed x1, local copies, waits for them, and re-layouts  2.26 us

profile of v2, /device:TPU:0, one launch (start us, length us, event | category | flops | bytes accessed | tf_op | source)
XLA Modules:
  0.0 40.7 jit_solution(2247384250869785920)
XLA Ops:
  0.7 37.8 %shard_map.100 = bf16[512,1024]{1,0:T(8,128)(2,1)} custom-call(s32[1]{0:T(128)S(6)} %copy.12.counts, bf16[512,1024]{1,0:T(8,128)(2,1)} %points_hbm.1, bf16[512,1024]{1,0:T(8,128)(2,1)} %cot_hbm.1, bf16[1024,1024]{1,0:T(8,128)(2,1)} %wq_hbm.1, bf16[1024,1024]{1,0:T(8,128)(2,1)} %wk_hbm.1, bf16[1024,1024]{1,0:T(8,128)(2,1)} %wv_hbm.1, f32[1,1024]{1,0:T(1,128)} %bitcast.4, ...), custom_call_target="tpu_custom_call" | custom-call | flops 6442450944 | bytes 12582912 | tf_op jit(solution)/shard_map/pallas_call | solution.py:331
  38.4 2.3 %copy.13 = bf16[512,1024]{1,0:T(8,128)(2,1)} copy(bf16[512,1024]{1,0:T(8,128)(2,1)} %shard_map.100) | data formatting | bytes 2097152
